TPU v7x, 32 devices: a whole 2x2x4 slice. The times are simulated.
32 devices in a mesh: contour: 4 (over y, x), clus: 8 (over z, core).
Axes of the slice: x: 2, y: 2, z: 4, core: 2. Of those that a mesh axis runs over, the one named last changes fastest.
Arguments:
- probes: float32 [64, 2, 16, 128], P('clus'), may hold values from -18 to 18
- near_blocks: bfloat16 [256, 27, 2, 128, 128], P(('contour', 'clus')), parts along dimension 0
- near_list: int32 [64, 27], P('clus'), may hold values from 0 to 63, as said below
- near_count: int32 [64], P('clus'), may hold values from 1 to 27
- cluster_rows: int32 [64], P('clus'), may hold values from 64 to 128
- row_basis: bfloat16 [256, 2, 32, 128], P(('contour', 'clus')), parts along dimension 0, may hold values from -1 to 1
- col_basis: bfloat16 [256, 2, 32, 128], P(('contour', 'clus')), parts along dimension 0, may hold values from -0.5 to 0.5
- far_list: int32 [64, 32], P('clus'), may hold values from 0 to 63, as said below
- far_coupling: float32 [256, 32, 2, 32, 32], P(('contour', 'clus')), parts along dimension 0, may hold values from -0.375 to 0.375
- weight: float32 [8], P('contour'), parts along dimension 0, may hold values from -6 to 6
Outputs:
- solution: float32 [256, 2, 16, 128], P(('contour', 'clus')), parts along dimension 0
- moment: float32 [8, 16, 16], P('contour'), parts along dimension 0
- arnoldi: float32 [16, 16], P('contour'), parts along dimension 0
There are 4 independent parts, one for each index of `contour`. A program takes and returns all parts, laid end to end along the dimension named above; an argument that names none is the same for every part. Nothing has to cross between parts.
Inputs may be any that keep to these rules, and one draw needn't show every extreme that they name: near_list[i, 0] = i; every entry lies within 8 clusters of i. `far_list`: every entry j of cluster i's list has min(|j - i|, 64 - |j - i|) > 8, so no far slot names a cluster of i's near list.
All inputs are finite; a program needn't handle non-finite values.
Results may differ from a plain program's by a relative error of at most 0.0019.
Values may be sent and summed in bfloat16 or wider, within the bound.
A program may use at most 128 MiB of HBM per device.

v0:
```python
import jax
import jax.numpy as jnp
from jax import lax
from jax.sharding import PartitionSpec as P


def padded_2(cells, sides, width):
    for axis, dim in sides:
        count = lax.axis_size(axis)
        ends = count - 1
        head = lax.slice_in_dim(cells, 0, width, axis=dim)
        tail = lax.slice_in_dim(cells, cells.shape[dim] - width, cells.shape[dim], axis=dim)
        cells = jnp.concatenate(
            [
                lax.ppermute(tail, axis, [(i, (i + 1) % count) for i in range(ends)]),
                cells,
                lax.ppermute(head, axis, [((i + 1) % count, i) for i in range(ends)]),
            ],
            axis=dim,
        )
    return cells


def block_product(blocks, pulled):

    def prod(mat, vec):
        return jnp.einsum("nkrs,nkps->npr", mat, vec, preferred_element_type=jnp.float32)

    real_part = prod(blocks[:, :, 0], pulled[:, :, 0]) - prod(blocks[:, :, 1], pulled[:, :, 1])
    imag_part = prod(blocks[:, :, 0], pulled[:, :, 1]) + prod(blocks[:, :, 1], pulled[:, :, 0])
    return jnp.stack([real_part, imag_part], axis=1)


def basis_contract(basis, narrow):

    def contract(mat, vec):
        return jnp.einsum("nqr,npr->nqp", mat, vec, preferred_element_type=jnp.float32)

    real_part = contract(basis[:, 0], narrow[:, 0]) - contract(basis[:, 1], narrow[:, 1])
    imag_part = contract(basis[:, 0], narrow[:, 1]) + contract(basis[:, 1], narrow[:, 0])
    count = real_part.shape[0]
    return jnp.stack([real_part.reshape(count, -1), imag_part.reshape(count, -1)], axis=1)


def basis_expand(basis, farcoef):

    def expand(mat, vec):
        return jnp.einsum("nqr,nqp->npr", mat, vec, preferred_element_type=jnp.float32)

    real_part = expand(basis[:, 0], farcoef[:, 0]) - expand(basis[:, 1], farcoef[:, 1])
    imag_part = expand(basis[:, 0], farcoef[:, 1]) + expand(basis[:, 1], farcoef[:, 0])
    return jnp.stack([real_part, imag_part], axis=1)


def far_couple(coupling, taken):
    high = lax.Precision.HIGHEST

    def couple(mat, vec):
        return jnp.einsum("nfqs,nfsp->nqp", mat, vec, precision=high)

    real_part = couple(coupling[:, :, 0], taken[:, :, 0]) - couple(
        coupling[:, :, 1], taken[:, :, 1]
    )
    imag_part = couple(coupling[:, :, 0], taken[:, :, 1]) + couple(
        coupling[:, :, 1], taken[:, :, 0]
    )
    return jnp.stack([real_part, imag_part], axis=1)


def inner(left, right):
    real_part = jnp.sum(left[:, 0] * right[:, 0] + left[:, 1] * right[:, 1], axis=(0, 2))
    imag_part = jnp.sum(left[:, 0] * right[:, 1] - left[:, 1] * right[:, 0], axis=(0, 2))
    return (real_part, imag_part)


def squares(field):
    return jnp.sum(field * field, axis=(0, 1, 3))


def scaled(field, real_part, imag_part):
    sr = real_part[None, :, None]
    si = imag_part[None, :, None]
    return jnp.stack(
        [sr * field[:, 0] - si * field[:, 1], sr * field[:, 1] + si * field[:, 0]], axis=1
    )


def shards(
    probes,
    near_blocks,
    near_list,
    near_count,
    cluster_rows,
    row_basis,
    col_basis,
    far_list,
    far_coupling,
    weight,
):
    owned = probes.shape[0]
    nprobe = probes.shape[2]
    width = probes.shape[3]
    rank = col_basis.shape[2]
    first_id = lax.axis_index("clus") * owned
    total_clusters = owned * lax.axis_size("clus")
    rows_iota = lax.broadcasted_iota(jnp.int32, (owned, width), 1)
    row_mask = (rows_iota < cluster_rows[:, None]).astype(jnp.float32)[:, None, None, :]
    slots_iota = lax.broadcasted_iota(jnp.int32, near_list.shape, 1)
    slot_live = slots_iota < near_count[:, None]
    local_ids = near_list - (first_id - owned)

    def operate(field):
        narrow = field.astype(jnp.bfloat16)
        padded = padded_2(narrow, (("clus", 0),), owned)
        pulled = jnp.take(padded, local_ids, axis=0)
        pulled = jnp.where(slot_live[:, :, None, None, None], pulled, jnp.zeros((), jnp.bfloat16))
        near = block_product(near_blocks, pulled)
        coef = basis_contract(col_basis, narrow)
        whole = lax.all_gather(coef, "clus", axis=0, tiled=True)
        whole = whole.reshape(whole.shape[0], 2, rank, nprobe)
        taken = jnp.take(whole, far_list, axis=0)
        farcoef = far_couple(far_coupling, taken)
        farcoef_b = farcoef.astype(jnp.bfloat16)
        far = basis_expand(row_basis, farcoef_b)
        return (near + far) * row_mask

    base = probes * row_mask
    beta = jnp.sqrt(lax.psum(squares(base), "clus") + 1e-06)
    first = base / beta[None, None, :, None]
    image_one = operate(first)
    local_re, local_im = inner(first, image_one)
    proj_re, proj_im = lax.psum((local_re, local_im), "clus")
    remain = image_one - scaled(first, proj_re, proj_im)
    norm_sq = lax.psum(squares(remain), "clus")
    size_two = jnp.sqrt(norm_sq + 1e-06)
    second = remain / size_two[None, None, :, None]
    factor = 1.0 / (total_clusters * width)
    arnoldi = jnp.stack([beta * jnp.sqrt(jnp.float32(factor)), proj_re, proj_im, size_two], axis=0)
    image_two = operate(second)
    g12r, g12i = inner(image_one, image_two)
    q1r, q1i = inner(image_one, base)
    q2r, q2i = inner(image_two, base)
    g11, g22, g12r, g12i, q1r, q1i, q2r, q2i = lax.psum(
        (squares(image_one), squares(image_two), g12r, g12i, q1r, q1i, q2r, q2i), "clus"
    )
    det = g11 * g22 - (g12r * g12r + g12i * g12i)
    y1r = (g22 * q1r - (g12r * q2r - g12i * q2i)) / det
    y1i = (g22 * q1i - (g12r * q2i + g12i * q2r)) / det
    y2r = (g11 * q2r - (g12r * q1r + g12i * q1i)) / det
    y2i = (g11 * q2i - (g12r * q1i - g12i * q1r)) / det
    iterate = scaled(first, y1r, y1i) + scaled(second, y2r, y2i)
    wr = weight[0]
    wi = weight[1]
    solution = jnp.stack(
        [wr * iterate[:, 0] - wi * iterate[:, 1], wr * iterate[:, 1] + wi * iterate[:, 0]], axis=1
    )
    high = lax.Precision.HIGHEST
    mom_re = jnp.einsum("npr,nqr->pq", base[:, 0], iterate[:, 0], precision=high) + jnp.einsum(
        "npr,nqr->pq", base[:, 1], iterate[:, 1], precision=high
    )
    mom_im = jnp.einsum("npr,nqr->pq", base[:, 0], iterate[:, 1], precision=high) - jnp.einsum(
        "npr,nqr->pq", base[:, 1], iterate[:, 0], precision=high
    )
    mom_re, mom_im = lax.psum((mom_re, mom_im), "clus")
    moment = jnp.stack([wr * mom_re - wi * mom_im, wr * mom_im + wi * mom_re], axis=0) * factor
    return (solution, moment, arnoldi)


def solution(mesh):
    in_specs = (
        P("clus", None, None, None),
        P(("contour", "clus"), None, None, None, None),
        P("clus", None),
        P("clus"),
        P("clus"),
        P(("contour", "clus"), None, None, None),
        P(("contour", "clus"), None, None, None),
        P("clus", None),
        P(("contour", "clus"), None, None, None, None),
        P("contour"),
    )
    out_specs = (
        P(("contour", "clus"), None, None, None),
        P("contour", None, None),
        P("contour", None),
    )
    return jax.shard_map(shards, mesh=mesh, in_specs=in_specs, out_specs=out_specs, check_vma=False)
```

profile of v0, /device:TPU:0, one launch (start us, length us, event | category | flops | bytes accessed | tf_op | source)
XLA Modules:
  0.0 235.3 jit_solution(8270889737625349476)
XLA Ops:
  0.6 0.7 fusion.208
  1.4 1.0 multiply_reduce_fusion.3
  2.4 18.2 %psum.98 = f32[16]{0:T(128)S(1)} all-reduce(f32[16]{0:T(128)S(1)} %get-tuple-element.43), channel_id=1, replica_groups=mesh['contour'=4,'clus'=8] {'clus'}, use_global_device_ids=true, to_apply=%region_1.0 | all-reduce | flops 16 | bytes 128 | tf_op jit(solution)/shard_map/psum | solution.py:128
  20.7 1.3 collective-permute-start.1
  22.0 3.0 %collective-permute-start = (bf16[8,2,16,128]{3,2,0,1:T(8,128)(2,1)S(1)}, bf16[8,2,16,128]{3,2,0,1:T(8,128)(2,1)S(1)}, u32[]{:S(2)}, u32[]{:S(2)}) collective-permute-start(bf16[8,2,16,128]{3,2,0,1:T(8,128)(2,1)S(1)} %get-tuple-element.41), channel_id=1, source_target_pairs={{0,1},{1,2},{2,3},{3,4},{4,5},{5,6},{6,7},{8,9},{9,10},{10,11},{11... | collective-permute-start | bytes 196616 | tf_op jit(solution)/shard_map/ppermute | solution.py:15
  25.0 1.0 fusion.176
  26.0 1.0 fusion.178
  27.0 0.7 compare_select_fusion.1
  27.7 0.7 compare_and_fusion.1
  28.4 1.0 fusion.78
  29.6 1.0 fusion.79
  30.8 14.2 %all_gather.6 = f32[64,2,512]{2,0,1:T(8,128)S(1)} all-gather(f32[8,2,512]{2,0,1:T(8,128)S(1)} %pad_maximum_fusion.3), channel_id=1, replica_groups=mesh['contour'=4,'clus'=8] {'clus'}, dimensions={0}, use_global_device_ids=true | all-gather | bytes 294912 | tf_op jit(solution)/shard_map/all_gather | solution.py:119
  45.0 0.2 copy.33
  45.2 1.0 copy.34
  46.3 3.0 %gather_fusion.1 = f32[256,2,32,16]{2,3,1,0:T(8,128)} fusion(f32[64,2,32,16]{2,3,1,0:T(8,128)S(1)} %copy.34, s32[1024]{0:T(1024)S(1)} %pad_clamp_fusion), kind=kCustom, calls=%fused_computation.1.clone | custom fusion | bytes 2098176 | tf_op jit(solution)/shard_map/jit(_take)/gather | solution.py:121
  49.3 2.6 %copy.35 = f32[256,2,32,16]{2,3,0,1:T(8,128)S(1)} copy(f32[256,2,32,16]{2,3,1,0:T(8,128)} %gather_fusion.1) | data formatting | bytes 2097152 | tf_op jit(solution)/shard_map/jit(_take)/gather | solution.py:121
  51.9 0.7 broadcast_select_fusion.1
  52.7 1.6 slice-done.1
  54.3 3.7 %fusion.83 = f32[8,16,32]{2,1,0:T(8,128)S(1)} fusion(f32[8,32,2,32,32]{4,3,2,1,0:T(8,128)S(1)} %bitcast.475, f32[8,32,2,32,16]{3,4,1,0,2:T(8,128)S(1)} %broadcast_select_fusion.1), kind=kOutput, calls=%fused_computation.85 | convolution fusion | flops 50331648 | bytes 6307840 | tf_op jit(solution)/shard_map/nfqs,nfsp->nqp/dot_general | solution.py:59
  58.1 3.7 %fusion.80 = f32[8,16,32]{2,1,0:T(8,128)S(1)} fusion(f32[8,32,2,32,32]{4,3,2,1,0:T(8,128)S(1)} %bitcast.475, f32[8,32,2,32,16]{3,4,1,0,2:T(8,128)S(1)} %broadcast_select_fusion.1), kind=kOutput, calls=%fused_computation.84 | convolution fusion | flops 50331648 | bytes 6307840 | tf_op jit(solution)/shard_map/nfqs,nfsp->nqp/dot_general | solution.py:59
  61.9 6.7 %fusion.143 = bf16[8,16,32]{2,1,0:T(8,128)(2,1)S(1)} fusion(f32[8,16,32]{2,1,0:T(8,128)S(1)} %fusion.83, f32[8,32,2,32,32]{4,3,2,1,0:T(8,128)} %param.22, f32[8,32,2,32,16]{3,4,1,0,2:T(8,128)} %copy-done), kind=kOutput, calls=%fused_computation.105 | convolution fusion | flops 50339840 | bytes 6316032 | tf_op jit(solution)/shard_map/nfqs,nfsp->nqp/dot_general | solution.py:59
  68.7 5.7 %fusion.140 = bf16[8,16,32]{2,1,0:T(8,128)(2,1)S(1)} fusion(f32[8,16,32]{2,1,0:T(8,128)S(1)} %fusion.80, f32[8,32,2,32,32]{4,3,2,1,0:T(8,128)} %param.22, f32[8,32,2,32,16]{3,4,1,0,2:T(8,128)S(1)} %copy-done.1), kind=kOutput, calls=%fused_computation.104 | convolution fusion | flops 50339840 | bytes 6365184 | tf_op jit(solution)/shard_map/nfqs,nfsp->nqp/dot_general | solution.py:59
  75.0 0.7 fusion.213
  75.7 1.0 gather_fusion
  76.7 0.3 copy.26
  77.0 0.7 select_select_fusion.1
  77.7 5.2 %fusion.51 = f32[8,16,128]{2,1,0:T(8,128)S(1)} fusion(bf16[8,27,2,128,128]{4,3,2,1,0:T(8,128)(2,1)} %param.15, bf16[8,27,2,16,128]{4,3,1,0,2:T(8,128)(2,1)S(1)} %select_select_fusion.1), kind=kOutput, calls=%fused_computation.61 | convolution fusion | flops 113246208 | bytes 8028160 | tf_op jit(solution)/shard_map/nkrs,nkps->npr/dot_general | solution.py:27
  82.9 5.2 %fusion.48 = f32[8,16,128]{2,1,0:T(8,128)S(1)} fusion(bf16[8,27,2,128,128]{4,3,2,1,0:T(8,128)(2,1)} %param.15, bf16[8,27,2,16,128]{4,3,1,0,2:T(8,128)(2,1)S(1)} %select_select_fusion.1), kind=kOutput, calls=%fused_computation.60 | convolution fusion | flops 113246208 | bytes 8028160 | tf_op jit(solution)/shard_map/nkrs,nkps->npr/dot_general | solution.py:27
  88.1 5.2 %fusion.119 = f32[8,1,16,128]{3,2,0,1:T(8,128)S(1)} fusion(f32[8,16,128]{2,1,0:T(8,128)S(1)} %fusion.51, bf16[8,27,2,128,128]{4,3,2,1,0:T(8,128)(2,1)} %param.15, bf16[8,27,2,16,128]{4,3,1,0,2:T(8,128)(2,1)S(1)} %select_select_fusion.1), kind=kOutput, calls=%fused_computation.97 | convolution fusion | flops 113262592 | bytes 8093696 | tf_op jit(solution)/shard_map/nkrs,nkps->npr/dot_general | solution.py:27
  93.4 2.0 fusion.125
  95.5 13.9 %all-reduce.2 = (f32[16]{0:T(128)S(1)}, f32[16]{0:T(128)S(1)}) all-reduce(f32[16]{0:T(128)S(1)} %get-tuple-element.18, f32[16]{0:T(128)S(1)} %get-tuple-element.17), channel_id=1, replica_groups=mesh['contour'=4,'clus'=8] {'clus'}, use_global_device_ids=true, to_apply=%region_5.8 | all-reduce | flops 32 | bytes 256 | tf_op jit(solution)/shard_map/psum | solution.py:132
  109.7 13.6 %psum.101 = f32[16]{0:T(128)S(1)} all-reduce(f32[16]{0:T(128)S(1)} %get-tuple-element.22), channel_id=1, replica_groups=mesh['contour'=4,'clus'=8] {'clus'}, use_global_device_ids=true, to_apply=%region_7.10 | all-reduce | flops 16 | bytes 128 | tf_op jit(solution)/shard_map/psum | solution.py:134
  124.5 14.2 %all_gather.7 = f32[64,2,512]{2,0,1:T(8,128)S(1)} all-gather(f32[8,2,512]{2,0,1:T(8,128)S(1)} %pad_maximum_fusion.4), channel_id=1, replica_groups=mesh['contour'=4,'clus'=8] {'clus'}, dimensions={0}, use_global_device_ids=true | all-gather | bytes 294912 | tf_op jit(solution)/shard_map/all_gather | solution.py:119
  138.7 0.2 copy.43
  138.9 1.0 copy.44
  139.9 3.0 %gather_fusion.3 = f32[256,2,32,16]{2,3,1,0:T(8,128)} fusion(f32[64,2,32,16]{2,3,1,0:T(8,128)S(1)} %copy.44, s32[1024]{0:T(1024)S(1)} %pad_clamp_fusion), kind=kCustom, calls=%fused_computation.3.clone | custom fusion | bytes 2098176 | tf_op jit(solution)/shard_map/jit(_take)/gather | solution.py:121
  142.9 2.6 %copy.45 = f32[256,2,32,16]{2,3,0,1:T(8,128)S(1)} copy(f32[256,2,32,16]{2,3,1,0:T(8,128)} %gather_fusion.3) | data formatting | bytes 2097152 | tf_op jit(solution)/shard_map/jit(_take)/gather | solution.py:121
  145.5 0.7 broadcast_select_fusion
  146.3 1.6 slice-done.3
  147.9 3.7 %fusion.89 = f32[8,16,32]{2,1,0:T(8,128)S(1)} fusion(f32[8,32,2,32,32]{4,3,2,1,0:T(8,128)S(1)} %bitcast.477, f32[8,32,2,32,16]{3,4,1,0,2:T(8,128)S(1)} %broadcast_select_fusion), kind=kOutput, calls=%fused_computation.87 | convolution fusion | flops 50331648 | bytes 6307840 | tf_op jit(solution)/shard_map/nfqs,nfsp->nqp/dot_general | solution.py:59
  151.6 3.7 %fusion.86 = f32[8,16,32]{2,1,0:T(8,128)S(1)} fusion(f32[8,32,2,32,32]{4,3,2,1,0:T(8,128)S(1)} %bitcast.477, f32[8,32,2,32,16]{3,4,1,0,2:T(8,128)S(1)} %broadcast_select_fusion), kind=kOutput, calls=%fused_computation.86 | convolution fusion | flops 50331648 | bytes 6307840 | tf_op jit(solution)/shard_map/nfqs,nfsp->nqp/dot_general | solution.py:59
  155.3 1.3 collective-permute-start.3
  156.6 3.5 %collective-permute-start.2 = (bf16[8,2,16,128]{3,2,0,1:T(8,128)(2,1)S(1)}, bf16[8,2,16,128]{3,2,0,1:T(8,128)(2,1)S(1)}, u32[]{:S(2)}, u32[]{:S(2)}) collective-permute-start(bf16[8,2,16,128]{3,2,0,1:T(8,128)(2,1)S(1)} %get-tuple-element.37), channel_id=1, source_target_pairs={{0,1},{1,2},{2,3},{3,4},{4,5},{5,6},{6,7},{8,9},{9,10},{10,11},{11... | collective-permute-start | bytes 196616 | tf_op jit(solution)/shard_map/ppermute | solution.py:15
  160.1 3.7 %fusion.149 = bf16[8,16,32]{2,1,0:T(8,128)(2,1)S(1)} fusion(f32[8,16,32]{2,1,0:T(8,128)S(1)} %fusion.89, f32[8,32,2,32,32]{4,3,2,1,0:T(8,128)S(1)} %bitcast.477, f32[8,32,2,32,16]{3,4,1,0,2:T(8,128)S(1)} %broadcast_select_fusion), kind=kOutput, calls=%fused_computation.107 | convolution fusion | flops 50339840 | bytes 6365184 | tf_op jit(solution)/shard_map/nfqs,nfsp->nqp/dot_general | solution.py:59
  164.0 3.7 %fusion.146 = bf16[8,16,32]{2,1,0:T(8,128)(2,1)S(1)} fusion(f32[8,16,32]{2,1,0:T(8,128)S(1)} %fusion.86, f32[8,32,2,32,32]{4,3,2,1,0:T(8,128)S(1)} %bitcast.477, f32[8,32,2,32,16]{3,4,1,0,2:T(8,128)S(1)} %broadcast_select_fusion), kind=kOutput, calls=%fused_computation.106 | convolution fusion | flops 50339840 | bytes 6365184 | tf_op jit(solution)/shard_map/nfqs,nfsp->nqp/dot_general | solution.py:59
  168.2 0.6 pad_maximum_fusion.5
  168.8 1.0 gather_fusion.2
  169.8 0.3 copy.40
  170.1 0.8 select_select_fusion
  171.0 5.2 %fusion.57 = f32[8,16,128]{2,1,0:T(8,128)S(1)} fusion(bf16[8,27,2,128,128]{4,3,2,1,0:T(8,128)(2,1)} %param.15, bf16[8,27,2,16,128]{4,3,1,0,2:T(8,128)(2,1)S(1)} %select_select_fusion), kind=kOutput, calls=%fused_computation.63 | convolution fusion | flops 113246208 | bytes 8028160 | tf_op jit(solution)/shard_map/nkrs,nkps->npr/dot_general | solution.py:27
  176.2 5.2 %fusion.54 = f32[8,16,128]{2,1,0:T(8,128)S(1)} fusion(bf16[8,27,2,128,128]{4,3,2,1,0:T(8,128)(2,1)} %param.15, bf16[8,27,2,16,128]{4,3,1,0,2:T(8,128)(2,1)S(1)} %select_select_fusion), kind=kOutput, calls=%fused_computation.62 | convolution fusion | flops 113246208 | bytes 8028160 | tf_op jit(solution)/shard_map/nkrs,nkps->npr/dot_general | solution.py:27
  181.4 5.2 %fusion.107 = f32[8,1,16,128]{3,2,0,1:T(8,128)S(1)} fusion(f32[8,16,128]{2,1,0:T(8,128)S(1)} %fusion.57, bf16[8,27,2,128,128]{4,3,2,1,0:T(8,128)(2,1)} %param.15, bf16[8,27,2,16,128]{4,3,1,0,2:T(8,128)(2,1)S(1)} %select_select_fusion), kind=kOutput, calls=%fused_computation.93 | convolution fusion | flops 113262592 | bytes 8093696 | tf_op jit(solution)/shard_map/nkrs,nkps->npr/dot_general | solution.py:27
  186.6 2.0 fusion.113
  188.7 0.2 add_reduce_fusion.2
  189.0 15.2 %all-reduce.1 = (f32[16]{0:T(128)S(1)}, f32[16]{0:T(128)S(1)}, f32[16]{0:T(128)S(1)}, f32[16]{0:T(128)S(1)}, f32[16]{0:T(128)S(1)}, /*index=5*/f32[16]{0:T(128)S(1)}, f32[16]{0:T(128)S(1)}, f32[16]{0:T(128)S(1)}) all-reduce(f32[16]{0:T(128)S(1)} %get-tuple-element.45, ...), channel_id=1, replica_groups=mesh['contour'=4,'clus'=8] {'clus'}, use_global_device_ids=true, to_apply=%region_17.20 | all-reduce | flops 128 | bytes 1024 | tf_op jit(solution)/shard_map/psum | solution.py:143
  204.4 0.2 convolution_bitcast_fusion.2
  204.5 0.2 convolution_bitcast_fusion
  204.8 1.4 multiply_subtract_fusion
  206.2 0.7 copy.46
  206.8 0.2 fusion.152
  207.0 0.2 fusion.153
  207.2 26.0 %all-reduce = (f32[16,16]{1,0:T(8,128)S(1)}, f32[16,16]{1,0:T(8,128)S(1)}) all-reduce(f32[16,16]{1,0:T(8,128)S(1)} %fusion.152, f32[16,16]{1,0:T(8,128)S(1)} %fusion.153), channel_id=1, replica_groups=mesh['contour'=4,'clus'=8] {'clus'}, use_global_device_ids=true, to_apply=%region_24.27 | all-reduce | flops 512 | bytes 4096 | tf_op jit(solution)/shard_map/psum | solution.py:164
  233.2 1.3 subtract_bitcast_fusion
  234.5 0.6 maximum_multiply_fusion
  (87 shorter events, 4.2 us)
Async XLA Ops:
  20.7 55.0 %collective-permute-start.1 = (bf16[8,2,16,128]{3,2,0,1:T(8,128)(2,1)S(1)}, bf16[8,2,16,128]{3,2,0,1:T(8,128)(2,1)S(1)}, u32[]{:S(2)}, u32[]{:S(2)}) collective-permute-start(bf16[8,2,16,128]{3,2,0,1:T(8,128)(2,1)S(1)} %get-tuple-element.41), channel_id=1, source_target_pairs={{1,0},{2,1},{3,2},{4,3},{5,4},{6,5},{7,6},{9,8},{10,9},{11,10},{12... | collective-permute-start | bytes 196616 | tf_op jit(solution)/shard_map/ppermute | solution.py:17
  22.0 53.7 %collective-permute-start = (bf16[8,2,16,128]{3,2,0,1:T(8,128)(2,1)S(1)}, bf16[8,2,16,128]{3,2,0,1:T(8,128)(2,1)S(1)}, u32[]{:S(2)}, u32[]{:S(2)}) collective-permute-start(bf16[8,2,16,128]{3,2,0,1:T(8,128)(2,1)S(1)} %get-tuple-element.41), channel_id=1, source_target_pairs={{0,1},{1,2},{2,3},{3,4},{4,5},{5,6},{6,7},{8,9},{9,10},{10,11},{11... | collective-permute-start | bytes 196616 | tf_op jit(solution)/shard_map/ppermute | solution.py:15
  49.3 3.4 %slice-start = ((s8[8388608]{0:T(1024)(128)(4,1)}), s8[4194304]{0:T(1024)(128)(4,1)S(1)}, s32[]{:S(2)}) async-start(s8[8388608]{0:T(1024)(128)(4,1)} %bitcast.474), calls=%async_computation | async-start | bytes 8388608
  51.9 2.4 %slice-start.1 = ((s8[8388608]{0:T(1024)(128)(4,1)}), s8[4194304]{0:T(1024)(128)(4,1)S(1)}, s32[]{:S(2)}) async-start(s8[8388608]{0:T(1024)(128)(4,1)} %bitcast.474), calls=%async_computation.1 | async-start | bytes 8388608
  54.3 3.7 %copy-start = (f32[8,32,2,32,16]{3,4,1,0,2:T(8,128)}, f32[8,32,2,32,16]{3,4,1,0,2:T(8,128)S(1)}, u32[]{:S(2)}) copy-start(f32[8,32,2,32,16]{3,4,1,0,2:T(8,128)S(1)} %broadcast_select_fusion.1) | copy-start | bytes 3145732
  58.0 3.7 %copy-start.4 = (s32[8,27]{1,0:T(8,128)S(1)}, s32[8,27]{1,0:T(8,128)}, u32[]{:S(2)}) copy-start(s32[8,27]{1,0:T(8,128)} %param.16) | copy-start | bytes 2596
  58.0 3.7 %copy-start.6 = (s32[8]{0:T(128)S(1)}, s32[8]{0:T(128)}, u32[]{:S(2)}) copy-start(s32[8]{0:T(128)} %param.17) | copy-start | bytes 100
  61.9 6.7 %copy-start.1 = (f32[8,32,2,32,16]{3,4,1,0,2:T(8,128)S(1)}, f32[8,32,2,32,16]{3,4,1,0,2:T(8,128)}, u32[]{:S(2)}) copy-start(f32[8,32,2,32,16]{3,4,1,0,2:T(8,128)} %copy-done) | copy-start | bytes 3145732
  68.7 5.8 %copy-start.3 = (bf16[8,2,32,128]{3,2,1,0:T(8,128)(2,1)S(1)}, bf16[8,2,32,128]{3,2,1,0:T(8,128)(2,1)}, u32[]{:S(2)}) copy-start(bf16[8,2,32,128]{3,2,1,0:T(8,128)(2,1)} %param.19) | copy-start | bytes 393220
  68.7 6.3 %copy-start.5 = (f32[2]{0:T(128)S(1)}, f32[2]{0:T(128)}, u32[]{:S(2)}) copy-start(f32[2]{0:T(128)} %param.23) | copy-start | bytes 28
  77.7 15.6 %slice-start.4 = ((s8[14155776]{0:T(1024)(128)(4,1)}), s8[4194304]{0:T(1024)(128)(4,1)S(1)}, s32[]{:S(2)}) async-start(s8[14155776]{0:T(1024)(128)(4,1)} %bitcast.486), calls=%async_computation.4 | async-start | bytes 8388608
  77.7 15.6 %slice-start.5 = ((s8[14155776]{0:T(1024)(128)(4,1)}), s8[4194304]{0:T(1024)(128)(4,1)S(1)}, s32[]{:S(2)}) async-start(s8[14155776]{0:T(1024)(128)(4,1)} %bitcast.486), calls=%async_computation.5 | async-start | bytes 8388608
  82.9 10.4 %slice-start.6 = ((s8[14155776]{0:T(1024)(128)(4,1)}), s8[4194304]{0:T(1024)(128)(4,1)S(1)}, s32[]{:S(2)}) async-start(s8[14155776]{0:T(1024)(128)(4,1)} %bitcast.486), calls=%async_computation.6 | async-start | bytes 8388608
  88.1 5.2 %slice-start.7 = ((s8[14155776]{0:T(1024)(128)(4,1)}), s8[1572864]{0:T(1024)(128)(4,1)S(1)}, s32[]{:S(2)}) async-start(s8[14155776]{0:T(1024)(128)(4,1)} %bitcast.486), calls=%async_computation.7 | async-start | bytes 3145728
  93.3 30.1 %copy-start.2 = (bf16[8,2,32,128]{3,2,1,0:T(8,128)(2,1)S(1)}, bf16[8,2,32,128]{3,2,1,0:T(8,128)(2,1)}, u32[]{:S(2)}) copy-start(bf16[8,2,32,128]{3,2,1,0:T(8,128)(2,1)} %param.20) | copy-start | bytes 393220
  142.9 3.4 %slice-start.2 = ((s8[8388608]{0:T(1024)(128)(4,1)}), s8[4194304]{0:T(1024)(128)(4,1)S(1)}, s32[]{:S(2)}) async-start(s8[8388608]{0:T(1024)(128)(4,1)} %bitcast.476), calls=%async_computation.2 | async-start | bytes 8388608
  145.5 2.4 %slice-start.3 = ((s8[8388608]{0:T(1024)(128)(4,1)}), s8[4194304]{0:T(1024)(128)(4,1)S(1)}, s32[]{:S(2)}) async-start(s8[8388608]{0:T(1024)(128)(4,1)} %bitcast.476), calls=%async_computation.3 | async-start | bytes 8388608
  155.3 13.4 %collective-permute-start.3 = (bf16[8,2,16,128]{3,2,0,1:T(8,128)(2,1)S(1)}, bf16[8,2,16,128]{3,2,0,1:T(8,128)(2,1)S(1)}, u32[]{:S(2)}, u32[]{:S(2)}) collective-permute-start(bf16[8,2,16,128]{3,2,0,1:T(8,128)(2,1)S(1)} %get-tuple-element.37), channel_id=1, source_target_pairs={{1,0},{2,1},{3,2},{4,3},{5,4},{6,5},{7,6},{9,8},{10,9},{11,10},{12... | collective-permute-start | bytes 196616 | tf_op jit(solution)/shard_map/ppermute | solution.py:17
  156.6 12.1 %collective-permute-start.2 = (bf16[8,2,16,128]{3,2,0,1:T(8,128)(2,1)S(1)}, bf16[8,2,16,128]{3,2,0,1:T(8,128)(2,1)S(1)}, u32[]{:S(2)}, u32[]{:S(2)}) collective-permute-start(bf16[8,2,16,128]{3,2,0,1:T(8,128)(2,1)S(1)} %get-tuple-element.37), channel_id=1, source_target_pairs={{0,1},{1,2},{2,3},{3,4},{4,5},{5,6},{6,7},{8,9},{9,10},{10,11},{11... | collective-permute-start | bytes 196616 | tf_op jit(solution)/shard_map/ppermute | solution.py:15
  170.9 15.6 %slice-start.8 = ((s8[14155776]{0:T(1024)(128)(4,1)}), s8[4194304]{0:T(1024)(128)(4,1)S(1)}, s32[]{:S(2)}) async-start(s8[14155776]{0:T(1024)(128)(4,1)} %bitcast.488), calls=%async_computation.8 | async-start | bytes 8388608
  171.0 15.6 %slice-start.9 = ((s8[14155776]{0:T(1024)(128)(4,1)}), s8[4194304]{0:T(1024)(128)(4,1)S(1)}, s32[]{:S(2)}) async-start(s8[14155776]{0:T(1024)(128)(4,1)} %bitcast.488), calls=%async_computation.9 | async-start | bytes 8388608
  176.2 10.4 %slice-start.10 = ((s8[14155776]{0:T(1024)(128)(4,1)}), s8[4194304]{0:T(1024)(128)(4,1)S(1)}, s32[]{:S(2)}) async-start(s8[14155776]{0:T(1024)(128)(4,1)} %bitcast.488), calls=%async_computation.10 | async-start | bytes 8388608
  181.4 5.2 %slice-start.11 = ((s8[14155776]{0:T(1024)(128)(4,1)}), s8[1572864]{0:T(1024)(128)(4,1)S(1)}, s32[]{:S(2)}) async-start(s8[14155776]{0:T(1024)(128)(4,1)} %bitcast.488), calls=%async_computation.11 | async-start | bytes 3145728
where the time goes:
time: 239 us; the launch traced here: 235 us
  blocking collectives  115 us (48%)
  matrix products  76.3 us (32%)
  local copies, waits for them, and re-layouts  22 us (9%)
  other arithmetic  11.3 us (5%)
  starting transfers between devices  9.12 us (4%)
    dot_general x8, matrix products, prod(): jnp.einsum('nkrs,nkps->npr', mat, vec, preferred_element_type=jnp.float32)  35.1 us
    dot_general x8, matrix products, couple(): return jnp.einsum('nfqs,nfsp->nqp', mat, vec, precision=high)  34.7 us
    all_gather x2, blocking collectives, operate(): whole = lax.all_gather(coef, 'clus', axis=0, tiled=True)  28.4 us
    psum x1, blocking collectives, shards(): mom_re, mom_im = lax.psum((mom_re, mom_im), 'clus')  26 us
    psum x1, blocking collectives, shards(): beta = jnp.sqrt(lax.psum(squares(base), 'clus') + 1e-06)  18.2 us
    psum x1, blocking collectives, shards(): lax.psum((squares(image_one), squares(image_two), g12r, g12i, q1r, q1i, q...  15.2 us
    psum x1, blocking collectives, shards(): proj_re, proj_im = lax.psum((local_re, local_im), 'clus')  13.9 us
    psum x1, blocking collectives, shards(): norm_sq = lax.psum(squares(remain), 'clus')  13.6 us
  transfers between devices with their start and end apart: 4, of which 0 were waited for; matrix products, arithmetic and copies ran while one was open for 18% of the time, Pallas kernels for 0%

commit v1 on v0

v1 whole, which is shorter than its diff:
```python
import functools

import jax
import jax.numpy as jnp
from jax import lax
from jax.experimental import pallas as pl
from jax.experimental.pallas import tpu as pltpu
from jax.sharding import PartitionSpec as P

MESH = pl.DeviceIdType.MESH
F32 = jnp.float32
BF16 = jnp.bfloat16
BETA, PROJ, NORM, GRAM, COEF, HALO = 0, 1, 2, 3, 4, 6


def dot_nt(left, right, precision=None):
    return lax.dot_general(
        left, right, (((1,), (1,)), ((), ())), precision=precision, preferred_element_type=F32
    )


def joined(prod, half, lanes):
    re = prod[:half, :lanes] - prod[half:, lanes:]
    im = prod[half:, :lanes] + prod[:half, lanes:]
    return jnp.concatenate([re, im], axis=0)


def kernel(
    n,
    near_list,
    near_count,
    cluster_rows,
    far_list,
    weight,
    probes,
    row_basis,
    col_basis,
    near_hbm,
    far_hbm,
    solution_ref,
    moment_ref,
    arnoldi_ref,
    near_v,
    far_v,
    wide_hi,
    wide_lo,
    col_pad,
    xs,
    raw,
    spread,
    total,
    base,
    first,
    second,
    image_one,
    image_two,
    beta_s,
    proj_s,
    norm_s,
    gram_s,
    near_sem,
    far_sem,
    send_sem,
    recv_sem,
):
    owned, rows, width = probes.shape
    half = rows // 2
    slots = near_v.shape[1]
    fslots = far_v.shape[1]
    rank = far_v.shape[3]
    per = width // rank
    me = lax.axis_index("clus")

    def near_copy(i):
        return pltpu.make_async_copy(near_hbm.at[i], near_v.at[i], near_sem.at[i])

    def far_copy(i):
        return pltpu.make_async_copy(far_hbm.at[i], far_v.at[i], far_sem.at[i])

    for i in range(owned):
        far_copy(i).start()
    for i in range(owned):
        near_copy(i).start()

    barrier = pltpu.get_barrier_semaphore()
    for o in range(1, n):
        pl.semaphore_signal(
            barrier, inc=1, device_id={"clus": lax.rem(me + o, n)}, device_id_type=MESH
        )
    pl.semaphore_wait(barrier, n - 1)

    def share(buf, phase):
        def copy(slot, o):
            return pltpu.make_async_remote_copy(
                src_ref=buf.at[slot],
                dst_ref=buf.at[slot],
                send_sem=send_sem.at[phase, o],
                recv_sem=recv_sem.at[phase, o],
                device_id={"clus": lax.rem(me + o, n)},
                device_id_type=MESH,
            )

        for o in range(1, n):
            copy(me, o).start()

        def finish():
            for o in range(1, n):
                copy(lax.rem(me + n - o, n), o).wait_recv()
            for o in range(1, n):
                copy(me, o).wait_send()

        return finish

    def summed(buf):
        out = buf[0]
        for d in range(1, n):
            out = out + buf[d]
        return out

    def lane_sum(v):
        return jnp.sum(v, axis=1, keepdims=True)

    def square_part(ref):
        acc = jnp.zeros((rows, width), F32)
        for i in range(owned):
            v = ref[i]
            acc = acc + v * v
        return acc[:half] + acc[half:]

    def inner_part(left, right):
        re = jnp.zeros((half, width), F32)
        im = jnp.zeros((half, width), F32)
        for i in range(owned):
            lr, li = left[i, :half], left[i, half:]
            rr, ri = right[i, :half], right[i, half:]
            re = re + (lr * rr + li * ri)
            im = im + (lr * ri - li * rr)
        return re, im

    lane = lax.broadcasted_iota(jnp.int32, (rows, width), 1)
    for i in range(owned):
        base[i] = jnp.where(lane < cluster_rows[i], probes[i], 0.0)
    beta_s[me] = square_part(base)
    finish_beta = share(beta_s, BETA)

    col_pad[...] = jnp.zeros_like(col_pad)
    for i in range(owned):
        at = (i % per) * rank
        col_pad[i, at : at + rank] = col_basis[i, 0]
        col_pad[i, width + at : width + at + rank] = col_basis[i, 1]
    for op in range(2):
        xs[op, 3 * owned] = jnp.zeros((rows, width), BF16)

    def lay(i, carry):
        far_copy(i).wait()
        for g in range(fslots // per):
            for c in range(2):
                tile = jnp.concatenate([far_v[i, g * per + a, c] for a in range(per)], axis=1)
                hi = tile.astype(BF16)
                wide_hi[i, c, g] = hi
                wide_lo[i, c, g] = (tile - hi.astype(F32)).astype(BF16)
        return carry

    lax.fori_loop(0, owned, lay, 0)

    finish_beta()
    beta = jnp.sqrt(lane_sum(summed(beta_s)) + 1e-06)
    beta_rows = jnp.concatenate([beta, beta], axis=0)

    def operate(op, field, image, meanwhile):
        def halo(o, src, dst, to):
            return pltpu.make_async_remote_copy(
                src_ref=xs.at[op, pl.ds(src * owned, owned)],
                dst_ref=xs.at[op, pl.ds(dst * owned, owned)],
                send_sem=send_sem.at[HALO + op, o],
                recv_sem=recv_sem.at[HALO + op, o],
                device_id={"clus": to},
                device_id_type=MESH,
            )

        right, left = lax.rem(me + 1, n), lax.rem(me + n - 1, n)
        for i in range(owned):
            xs[op, owned + i] = field[i].astype(BF16)
        halo(0, 1, 0, right).start()
        halo(1, 1, 2, left).start()
        for g in range(owned // per):
            prod = jnp.zeros((rows, 2 * width), F32)
            for a in range(per):
                prod = prod + dot_nt(xs[op, owned + g * per + a], col_pad[g * per + a])
            raw[op, me, g] = joined(prod, half, width)
        finish_coef = share(raw.at[op], COEF + op)
        meanwhile()
        halo(0, 1, 0, right).wait_recv()
        halo(1, 1, 2, left).wait_recv()
        shift = (me - 1) * owned

        def near(i, carry):
            if op == 0:
                near_copy(i).wait()
            count = near_count[i]

            def pulled(k):
                at = jnp.where(k < count, near_list[i, k] - shift, 3 * owned)
                return xs[op, at]

            acc = jnp.zeros((rows, 2 * width), F32)
            for k in range(0, slots - 1, 2):
                lhs = jnp.concatenate([pulled(k), pulled(k + 1)], axis=1)
                rhs = jnp.concatenate([near_v[i, k], near_v[i, k + 1]], axis=1)
                acc = acc + dot_nt(lhs, rhs)
            if slots % 2:
                acc = acc + dot_nt(pulled(slots - 1), near_v[i, slots - 1])
            total[i] = acc
            return carry

        lax.fori_loop(0, owned, near, 0)
        finish_coef()

        def expand(d, carry):
            for g in range(owned // per):
                tile = raw[op, d, g]
                for a in range(per):
                    m = jnp.where((lane >= a * rank) & (lane < (a + 1) * rank), tile, 0.0)
                    step = width // 2
                    while step >= rank:
                        m = m + pltpu.roll(m, step, 1)
                        step //= 2
                    spread[d * owned + g * per + a] = m
            return carry

        lax.fori_loop(0, n, expand, 0)

        def far(i, carry):
            acc_r = jnp.zeros((rows, rank), F32)
            acc_i = jnp.zeros((rows, rank), F32)
            for g in range(fslots // per):
                t = spread[far_list[i, g * per]]
                for a in range(1, per):
                    t = jnp.where(lane >= a * rank, spread[far_list[i, g * per + a]], t)
                hi = t.astype(BF16)
                lo = (t - hi.astype(F32)).astype(BF16)
                wr, wi = wide_hi[i, 0, g], wide_hi[i, 1, g]
                acc_r = acc_r + (dot_nt(hi, wr) + (dot_nt(lo, wr) + dot_nt(hi, wide_lo[i, 0, g])))
                acc_i = acc_i + (dot_nt(hi, wi) + (dot_nt(lo, wi) + dot_nt(hi, wide_lo[i, 1, g])))
            fr = acc_r[:half] - acc_i[half:]
            fi = acc_r[half:] + acc_i[:half]
            coef = jnp.concatenate([fr, fi], axis=0).astype(BF16)
            basis = jnp.concatenate([row_basis[i, 0], row_basis[i, 1]], axis=1)
            prod = total[i] + jnp.dot(coef, basis, preferred_element_type=F32)
            image[i] = jnp.where(lane < cluster_rows[i], joined(prod, half, width), 0.0)
            return carry

        lax.fori_loop(0, owned, far, 0)
        halo(0, 1, 0, right).wait_send()
        halo(1, 1, 2, left).wait_send()

    for i in range(owned):
        first[i] = base[i] / beta_rows
    operate(0, first, image_one, lambda: None)

    re, im = inner_part(first, image_one)
    proj_s[me, :half] = re
    proj_s[me, half:] = im
    share(proj_s, PROJ)()
    proj = lane_sum(summed(proj_s))
    pr, pi = proj[:half], proj[half:]
    for i in range(owned):
        fr, fi = first[i, :half], first[i, half:]
        second[i, :half] = image_one[i, :half] - (pr * fr - pi * fi)
        second[i, half:] = image_one[i, half:] - (pr * fi + pi * fr)
    norm_s[me] = square_part(second)
    share(norm_s, NORM)()
    size_two = jnp.sqrt(lane_sum(summed(norm_s)) + 1e-06)
    size_rows = jnp.concatenate([size_two, size_two], axis=0)
    for i in range(owned):
        second[i] = second[i] / size_rows

    def moments():
        m1 = jnp.zeros((rows, rows), F32)
        m2 = jnp.zeros((rows, rows), F32)
        for i in range(owned):
            m1 = m1 + dot_nt(base[i], first[i], lax.Precision.HIGHEST)
            m2 = m2 + dot_nt(base[i], second[i], lax.Precision.HIGHEST)
        gram_s[me] = jnp.zeros(gram_s.shape[1:], F32)
        gram_s[me, half : half + rows, :rows] = m1
        gram_s[me, half + rows :, :rows] = m2

    operate(1, second, image_two, moments)

    parts = (
        square_part(image_one),
        square_part(image_two),
        *inner_part(image_one, image_two),
        *inner_part(image_one, base),
        *inner_part(image_two, base),
    )
    narrow = lax.broadcasted_iota(jnp.int32, (half, width), 1)
    packed = jnp.zeros((half, width), F32)
    for k, part in enumerate(parts):
        packed = jnp.where(narrow == k, lane_sum(part), packed)
    gram_s[me, :half] = packed
    share(gram_s, GRAM)()
    gram = summed(gram_s)
    g11, g22, g12r, g12i, q1r, q1i, q2r, q2i = (
        lane_sum(jnp.where(narrow == k, gram[:half], 0.0)) for k in range(8)
    )
    det = g11 * g22 - (g12r * g12r + g12i * g12i)
    y1r = (g22 * q1r - (g12r * q2r - g12i * q2i)) / det
    y1i = (g22 * q1i - (g12r * q2i + g12i * q2r)) / det
    y2r = (g11 * q2r - (g12r * q1r + g12i * q1i)) / det
    y2i = (g11 * q2i - (g12r * q1i - g12i * q1r)) / det
    wr, wi = weight[0], weight[1]
    y1r, y1i = wr * y1r - wi * y1i, wr * y1i + wi * y1r
    y2r, y2i = wr * y2r - wi * y2i, wr * y2i + wi * y2r
    for i in range(owned):
        fr, fi = first[i, :half], first[i, half:]
        sr, si = second[i, :half], second[i, half:]
        solution_ref[i, :half] = (y1r * fr - y1i * fi) + (y2r * sr - y2i * si)
        solution_ref[i, half:] = (y1r * fi + y1i * fr) + (y2r * si + y2i * sr)

    eye = lax.broadcasted_iota(jnp.int32, (half, half), 0) == lax.broadcasted_iota(
        jnp.int32, (half, half), 1
    )

    def as_row(column):
        return jnp.sum(jnp.where(eye, column, 0.0), axis=0, keepdims=True)

    factor = 1.0 / (n * owned * width)
    arnoldi_ref[0:1] = as_row(beta * jnp.sqrt(F32(factor)))
    arnoldi_ref[1:2] = as_row(pr)
    arnoldi_ref[2:3] = as_row(pi)
    arnoldi_ref[3:4] = as_row(size_two)

    def moment_of(m):
        re = m[:half, :half] + m[half:, half:rows]
        im = m[:half, half:rows] - m[half:, :half]
        return re, im

    m1r, m1i = moment_of(gram[half : half + rows])
    m2r, m2i = moment_of(gram[half + rows :])
    y1r, y1i, y2r, y2i = as_row(y1r), as_row(y1i), as_row(y2r), as_row(y2i)
    moment_ref[0] = ((y1r * m1r - y1i * m1i) + (y2r * m2r - y2i * m2i)) * factor
    moment_ref[1] = ((y1r * m1i + y1i * m1r) + (y2r * m2i + y2i * m2r)) * factor


def shards(
    n,
    probes,
    near_blocks,
    near_list,
    near_count,
    cluster_rows,
    row_basis,
    col_basis,
    far_list,
    far_coupling,
    weight,
):
    owned, _, nprobe, width = probes.shape
    rows = 2 * nprobe
    slots = near_blocks.shape[1]
    fslots = far_coupling.shape[1]
    rank = far_coupling.shape[3]
    per = width // rank
    groups = fslots // per
    smem = pl.BlockSpec(memory_space=pltpu.SMEM)
    vmem = pl.BlockSpec(memory_space=pltpu.VMEM)
    hbm = pl.BlockSpec(memory_space=pl.ANY)
    field = pltpu.VMEM((owned, rows, width), F32)
    sol, moment, arnoldi = pl.pallas_call(
        functools.partial(kernel, n),
        out_shape=(
            jax.ShapeDtypeStruct((owned, rows, width), F32),
            jax.ShapeDtypeStruct((2, nprobe, nprobe), F32),
            jax.ShapeDtypeStruct((4, nprobe), F32),
        ),
        in_specs=[smem] * 5 + [vmem] * 3 + [hbm] * 2,
        out_specs=(vmem, vmem, vmem),
        scratch_shapes=[
            pltpu.VMEM((owned, slots, 2 * width, width), BF16),
            pltpu.VMEM(far_coupling.shape, F32),
            pltpu.VMEM((owned, 2, groups, rank, width), BF16),
            pltpu.VMEM((owned, 2, groups, rank, width), BF16),
            pltpu.VMEM((owned, 2 * width, width), BF16),
            pltpu.VMEM((2, 3 * owned + 1, rows, width), BF16),
            pltpu.VMEM((2, n, owned // per, rows, width), F32),
            pltpu.VMEM((n * owned, rows, width), F32),
            pltpu.VMEM((owned, rows, 2 * width), F32),
            field,
            field,
            field,
            field,
            field,
            pltpu.VMEM((n, nprobe, width), F32),
            pltpu.VMEM((n, rows, width), F32),
            pltpu.VMEM((n, nprobe, width), F32),
            pltpu.VMEM((n, nprobe + 2 * rows, width), F32),
            pltpu.SemaphoreType.DMA((owned,)),
            pltpu.SemaphoreType.DMA((owned,)),
            pltpu.SemaphoreType.DMA((8, n)),
            pltpu.SemaphoreType.DMA((8, n)),
        ],
        compiler_params=pltpu.CompilerParams(
            collective_id=0, has_side_effects=True, vmem_limit_bytes=52 * 2**20
        ),
    )(
        near_list,
        near_count,
        cluster_rows,
        far_list,
        weight,
        probes.reshape(owned, rows, width),
        row_basis,
        col_basis,
        near_blocks.reshape(owned, slots, 2 * width, width),
        far_coupling,
    )
    return sol.reshape(probes.shape), moment, arnoldi


def solution(mesh):
    in_specs = (
        P("clus", None, None, None),
        P(("contour", "clus"), None, None, None, None),
        P("clus", None),
        P("clus"),
        P("clus"),
        P(("contour", "clus"), None, None, None),
        P(("contour", "clus"), None, None, None),
        P("clus", None),
        P(("contour", "clus"), None, None, None, None),
        P("contour"),
    )
    out_specs = (
        P(("contour", "clus"), None, None, None),
        P("contour", None, None),
        P("contour", None),
    )
    return jax.shard_map(
        functools.partial(shards, mesh.shape["clus"]),
        mesh=mesh,
        in_specs=in_specs,
        out_specs=out_specs,
        check_vma=False,
    )
```

time: 239 us -> 65.7 us (0.27); the launches traced: 235 us -> 64.9 us
  blocking collectives: 115 us -> 0 us
  matrix products: 76.3 us -> 0 us
  Pallas kernels: 0 us -> 56.4 us
  local copies, waits for them, and re-layouts: 22 us -> 7.88 us
  other arithmetic: 11.3 us -> 0 us
  starting transfers between devices: 9.12 us -> 0 us
    psum x5 -> x0, blocking collectives: 86.8 us -> none  [the longest x1 26 us: shards(): mom_re, mom_im = lax.psum((mom_re, mom_im), 'clus')]
    dot_general x36 -> x0, matrix products: 76.3 us -> none  [the longest x8 35.1 us: prod(): jnp.einsum('nkrs,nkps->npr', mat, vec, preferred_element_type=jnp.float32)]
    pallas_call x0 -> x1, Pallas kernels: none -> 56.4 us  [shards(): pl.pallas_call(functools.partial(kernel, n), out_shape=(jax.ShapeDtypeStr...]
    all_gather x2 -> x0, blocking collectives: 28.4 us -> none  [operate(): whole = lax.all_gather(coef, 'clus', axis=0, tiled=True)]
    gather x8 -> x0, local copies, waits for them, and re-layouts: 13.8 us -> none  [the longest x4 11.2 us: operate(): taken = jnp.take(whole, far_list, axis=0)]
    ppermute x4 -> x0, starting transfers between devices: 9.12 us -> none  [the longest x2 6.53 us: padded_2(): lax.ppermute(tail, axis, [(i, (i + 1) % count) for i in range(ends)])]
    unnamed x39 -> x19, local copies, waits for them, and re-layouts: 4.12 us -> 7.88 us
    select_n x5 -> x0, other arithmetic: 3.6 us -> none  [the longest x3 2.13 us: operate(): taken = jnp.take(whole, far_list, axis=0)]
  transfers between devices with their start and end apart: 4 -> 0, of which waited for: 0 -> 0; matrix products, arithmetic and copies ran while one was open for 18% -> 0% of each run, Pallas kernels for 0% -> 0%
where the time goes in v1:
time: 65.7 us; the launch traced here: 64.9 us
  Pallas kernels  56.4 us (86%)
  local copies, waits for them, and re-layouts  7.88 us (12%)
  between operations  0.66 us (1%)
    pallas_call x1, Pallas kernels, shards(): pl.pallas_call(functools.partial(kernel, n), out_shape=(jax.ShapeDtypeStr...  56.4 us
    unnamed x19, local copies, waits for them, and re-layouts  7.88 us

profile of v1, /device:TPU:0, one launch (start us, length us, event | category | flops | bytes accessed | tf_op | source)
XLA Modules:
  0.0 64.9 jit_solution(17000468098053632221)
XLA Ops:
  0.6 0.0 copy-start
  0.6 0.9 %copy-done = f32[8,2,16,128]{3,2,1,0:T(8,128)S(1)} copy-done((f32[8,2,16,128]{3,2,1,0:T(8,128)S(1)}, f32[8,2,16,128]{3,2,1,0:T(8,128)}, u32[]{:S(2)}) %copy-start) | copy-done | bytes 131096
  1.5 0.0 copy-start.1
  1.5 0.9 %copy-done.1 = bf16[8,2,32,128]{3,2,1,0:T(8,128)(2,1)S(1)} copy-done((bf16[8,2,32,128]{3,2,1,0:T(8,128)(2,1)S(1)}, bf16[8,2,32,128]{3,2,1,0:T(8,128)(2,1)}, u32[]{:S(2)}) %copy-start.1) | copy-done | bytes 131096
  2.4 0.0 copy-start.2
  2.4 0.9 %copy-done.2 = bf16[8,2,32,128]{3,2,1,0:T(8,128)(2,1)S(1)} copy-done((bf16[8,2,32,128]{3,2,1,0:T(8,128)(2,1)S(1)}, bf16[8,2,32,128]{3,2,1,0:T(8,128)(2,1)}, u32[]{:S(2)}) %copy-start.2) | copy-done | bytes 131096
  3.3 0.0 copy-start.3
  3.4 0.7 %copy-done.3 = s32[8,27]{1,0:T(8,128)S(1)} copy-done((s32[8,27]{1,0:T(8,128)S(1)}, s32[8,27]{1,0:T(8,128)}, u32[]{:S(2)}) %copy-start.3) | copy-done | bytes 888
  4.0 0.0 copy-start.4
  4.0 0.7 %copy-done.4 = s32[8,32]{1,0:T(8,128)S(1)} copy-done((s32[8,32]{1,0:T(8,128)S(1)}, s32[8,32]{1,0:T(8,128)}, u32[]{:S(2)}) %copy-start.4) | copy-done | bytes 1048
  4.7 0.0 copy-start.5
  4.7 0.7 %copy-done.5 = s32[8]{0:T(128)S(1)} copy-done((s32[8]{0:T(128)S(1)}, s32[8]{0:T(128)}, u32[]{:S(2)}) %copy-start.5) | copy-done | bytes 56
  5.4 0.0 copy-start.6
  5.4 0.7 %copy-done.6 = s32[8]{0:T(128)S(1)} copy-done((s32[8]{0:T(128)S(1)}, s32[8]{0:T(128)}, u32[]{:S(2)}) %copy-start.6) | copy-done | bytes 56
  6.0 0.0 copy-start.7
  6.0 0.7 %copy-done.7 = f32[2]{0:T(128)S(1)} copy-done((f32[2]{0:T(128)S(1)}, f32[2]{0:T(128)}, u32[]{:S(2)}) %copy-start.7) | copy-done | bytes 32
  6.7 56.4 %shard_map.121 = (f32[8,32,128]{2,1,0:T(8,128)S(1)}, f32[2,16,16]{2,1,0:T(8,128)S(1)}, f32[4,16]{1,0:T(4,128)S(1)}) custom-call(s32[8,27]{1,0:T(8,128)S(1)} %copy-done.3, s32[8]{0:T(128)S(1)} %copy-done.5, s32[8]{0:T(128)S(1)} %copy-done.6, s32[8,32]{1,0:T(8,128)S(1)} %copy-done.4, f32[2]{0:T(128)S(1)} %copy-done.7, f32[8,32,128]{2,1,0:T(8,128)S(1)} %bitcast.3, ...), custom_call_target="tpu_custom_call" | custom-call | tf_op jit(solution)/shard_map/pallas_call | solution.py:370
  63.1 0.7 %copy.16 = f32[8,2,16,128]{3,2,1,0:T(8,128)} copy(f32[8,2,16,128]{3,2,1,0:T(8,128)S(1)} %bitcast.4) | data formatting | bytes 262144
  63.7 0.6 copy.17
  64.3 0.6 copy.18
Async XLA Ops:
  0.6 0.9 %copy-start = (f32[8,2,16,128]{3,2,1,0:T(8,128)S(1)}, f32[8,2,16,128]{3,2,1,0:T(8,128)}, u32[]{:S(2)}) copy-start(f32[8,2,16,128]{3,2,1,0:T(8,128)} %param.10) | copy-start | bytes 393220
  1.5 0.9 %copy-start.1 = (bf16[8,2,32,128]{3,2,1,0:T(8,128)(2,1)S(1)}, bf16[8,2,32,128]{3,2,1,0:T(8,128)(2,1)}, u32[]{:S(2)}) copy-start(bf16[8,2,32,128]{3,2,1,0:T(8,128)(2,1)} %row_basis.1) | copy-start | bytes 393220
  2.4 0.9 %copy-start.2 = (bf16[8,2,32,128]{3,2,1,0:T(8,128)(2,1)S(1)}, bf16[8,2,32,128]{3,2,1,0:T(8,128)(2,1)}, u32[]{:S(2)}) copy-start(bf16[8,2,32,128]{3,2,1,0:T(8,128)(2,1)} %col_basis.1) | copy-start | bytes 393220
  3.3 0.7 %copy-start.3 = (s32[8,27]{1,0:T(8,128)S(1)}, s32[8,27]{1,0:T(8,128)}, u32[]{:S(2)}) copy-start(s32[8,27]{1,0:T(8,128)} %near_list.1) | copy-start | bytes 2596
  4.0 0.7 %copy-start.4 = (s32[8,32]{1,0:T(8,128)S(1)}, s32[8,32]{1,0:T(8,128)}, u32[]{:S(2)}) copy-start(s32[8,32]{1,0:T(8,128)} %far_list.1) | copy-start | bytes 3076
  4.7 0.7 %copy-start.5 = (s32[8]{0:T(128)S(1)}, s32[8]{0:T(128)}, u32[]{:S(2)}) copy-start(s32[8]{0:T(128)} %near_count.1) | copy-start | bytes 100
  5.4 0.7 %copy-start.6 = (s32[8]{0:T(128)S(1)}, s32[8]{0:T(128)}, u32[]{:S(2)}) copy-start(s32[8]{0:T(128)} %cluster_rows.1) | copy-start | bytes 100
  6.0 0.7 %copy-start.7 = (f32[2]{0:T(128)S(1)}, f32[2]{0:T(128)}, u32[]{:S(2)}) copy-start(f32[2]{0:T(128)} %weight.1) | copy-start | bytes 28

commit v2 on v1

--- a/solution.py
+++ b/solution.py
@@ -120,6 +120,16 @@
     def lane_sum(v):
         return jnp.sum(v, axis=1, keepdims=True)
 
+    eye = lax.broadcasted_iota(jnp.int32, (half, width), 0) == lax.broadcasted_iota(
+        jnp.int32, (half, width), 1
+    )
+
+    def as_row(column):
+        return jnp.sum(jnp.where(eye, column, 0.0), axis=0, keepdims=True)
+
+    def as_column(row):
+        return lane_sum(jnp.where(eye, row, 0.0))
+
     def square_part(ref):
         acc = jnp.zeros((rows, width), F32)
         for i in range(owned):
@@ -140,7 +150,7 @@
     lane = lax.broadcasted_iota(jnp.int32, (rows, width), 1)
     for i in range(owned):
         base[i] = jnp.where(lane < cluster_rows[i], probes[i], 0.0)
-    beta_s[me] = square_part(base)
+    beta_s[me] = as_row(lane_sum(square_part(base)))
     finish_beta = share(beta_s, BETA)
 
     col_pad[...] = jnp.zeros_like(col_pad)
@@ -157,14 +167,15 @@
             for c in range(2):
                 tile = jnp.concatenate([far_v[i, g * per + a, c] for a in range(per)], axis=1)
                 hi = tile.astype(BF16)
-                wide_hi[i, c, g] = hi
-                wide_lo[i, c, g] = (tile - hi.astype(F32)).astype(BF16)
+                to = slice(c * rank, (c + 1) * rank)
+                wide_hi[i, g, to] = hi
+                wide_lo[i, g, to] = (tile - hi.astype(F32)).astype(BF16)
         return carry
 
     lax.fori_loop(0, owned, lay, 0)
 
     finish_beta()
-    beta = jnp.sqrt(lane_sum(summed(beta_s)) + 1e-06)
+    beta = jnp.sqrt(as_column(summed(beta_s)) + 1e-06)
     beta_rows = jnp.concatenate([beta, beta], axis=0)
 
     def operate(op, field, image, meanwhile):
@@ -231,17 +242,25 @@
         lax.fori_loop(0, n, expand, 0)
 
         def far(i, carry):
-            acc_r = jnp.zeros((rows, rank), F32)
-            acc_i = jnp.zeros((rows, rank), F32)
-            for g in range(fslots // per):
+            acc_hi = jnp.zeros((2 * rows, 2 * rank), F32)
+            acc_lo = jnp.zeros((rows, 2 * rank), F32)
+
+            def taken(g):
                 t = spread[far_list[i, g * per]]
                 for a in range(1, per):
                     t = jnp.where(lane >= a * rank, spread[far_list[i, g * per + a]], t)
                 hi = t.astype(BF16)
                 lo = (t - hi.astype(F32)).astype(BF16)
-                wr, wi = wide_hi[i, 0, g], wide_hi[i, 1, g]
-                acc_r = acc_r + (dot_nt(hi, wr) + (dot_nt(lo, wr) + dot_nt(hi, wide_lo[i, 0, g])))
-                acc_i = acc_i + (dot_nt(hi, wi) + (dot_nt(lo, wi) + dot_nt(hi, wide_lo[i, 1, g])))
+                return jnp.concatenate([hi, lo], axis=0)
+
+            for g in range(0, fslots // per, 2):
+                both = jnp.concatenate([taken(g), taken(g + 1)], axis=1)
+                w_hi = jnp.concatenate([wide_hi[i, g], wide_hi[i, g + 1]], axis=1)
+                w_lo = jnp.concatenate([wide_lo[i, g], wide_lo[i, g + 1]], axis=1)
+                acc_hi = acc_hi + dot_nt(both, w_hi)
+                acc_lo = acc_lo + dot_nt(both[:rows], w_lo)
+            acc = acc_hi[:rows] + (acc_hi[rows:] + acc_lo)
+            acc_r, acc_i = acc[:, :rank], acc[:, rank:]
             fr = acc_r[:half] - acc_i[half:]
             fi = acc_r[half:] + acc_i[:half]
             coef = jnp.concatenate([fr, fi], axis=0).astype(BF16)
@@ -259,18 +278,18 @@
     operate(0, first, image_one, lambda: None)
 
     re, im = inner_part(first, image_one)
-    proj_s[me, :half] = re
-    proj_s[me, half:] = im
+    proj_s[me, 0:1] = as_row(lane_sum(re))
+    proj_s[me, 1:2] = as_row(lane_sum(im))
     share(proj_s, PROJ)()
-    proj = lane_sum(summed(proj_s))
-    pr, pi = proj[:half], proj[half:]
+    proj = summed(proj_s)
+    pr, pi = as_column(proj[0:1]), as_column(proj[1:2])
     for i in range(owned):
         fr, fi = first[i, :half], first[i, half:]
         second[i, :half] = image_one[i, :half] - (pr * fr - pi * fi)
         second[i, half:] = image_one[i, half:] - (pr * fi + pi * fr)
-    norm_s[me] = square_part(second)
+    norm_s[me] = as_row(lane_sum(square_part(second)))
     share(norm_s, NORM)()
-    size_two = jnp.sqrt(lane_sum(summed(norm_s)) + 1e-06)
+    size_two = jnp.sqrt(as_column(summed(norm_s)) + 1e-06)
     size_rows = jnp.concatenate([size_two, size_two], axis=0)
     for i in range(owned):
         second[i] = second[i] / size_rows
@@ -282,8 +301,10 @@
             m1 = m1 + dot_nt(base[i], first[i], lax.Precision.HIGHEST)
             m2 = m2 + dot_nt(base[i], second[i], lax.Precision.HIGHEST)
         gram_s[me] = jnp.zeros(gram_s.shape[1:], F32)
-        gram_s[me, half : half + rows, :rows] = m1
-        gram_s[me, half + rows :, :rows] = m2
+        for at, m in ((0, m1), (rows, m2)):
+            re = m[:half, :half] + m[half:, half:]
+            im = m[:half, half:] - m[half:, :half]
+            gram_s[me, :, at : at + rows] = jnp.concatenate([re, im], axis=1)
 
     operate(1, second, image_two, moments)
 
@@ -295,14 +316,14 @@
         *inner_part(image_two, base),
     )
     narrow = lax.broadcasted_iota(jnp.int32, (half, width), 1)
-    packed = jnp.zeros((half, width), F32)
+    packed = gram_s[me]
     for k, part in enumerate(parts):
-        packed = jnp.where(narrow == k, lane_sum(part), packed)
-    gram_s[me, :half] = packed
+        packed = jnp.where(narrow == 2 * rows + k, lane_sum(part), packed)
+    gram_s[me] = packed
     share(gram_s, GRAM)()
     gram = summed(gram_s)
     g11, g22, g12r, g12i, q1r, q1i, q2r, q2i = (
-        lane_sum(jnp.where(narrow == k, gram[:half], 0.0)) for k in range(8)
+        lane_sum(jnp.where(narrow == 2 * rows + k, gram, 0.0)) for k in range(8)
     )
     det = g11 * g22 - (g12r * g12r + g12i * g12i)
     y1r = (g22 * q1r - (g12r * q2r - g12i * q2i)) / det
@@ -318,27 +339,14 @@
         solution_ref[i, :half] = (y1r * fr - y1i * fi) + (y2r * sr - y2i * si)
         solution_ref[i, half:] = (y1r * fi + y1i * fr) + (y2r * si + y2i * sr)
 
-    eye = lax.broadcasted_iota(jnp.int32, (half, half), 0) == lax.broadcasted_iota(
-        jnp.int32, (half, half), 1
-    )
-
-    def as_row(column):
-        return jnp.sum(jnp.where(eye, column, 0.0), axis=0, keepdims=True)
-
     factor = 1.0 / (n * owned * width)
-    arnoldi_ref[0:1] = as_row(beta * jnp.sqrt(F32(factor)))
-    arnoldi_ref[1:2] = as_row(pr)
-    arnoldi_ref[2:3] = as_row(pi)
-    arnoldi_ref[3:4] = as_row(size_two)
-
-    def moment_of(m):
-        re = m[:half, :half] + m[half:, half:rows]
-        im = m[:half, half:rows] - m[half:, :half]
-        return re, im
-
-    m1r, m1i = moment_of(gram[half : half + rows])
-    m2r, m2i = moment_of(gram[half + rows :])
-    y1r, y1i, y2r, y2i = as_row(y1r), as_row(y1i), as_row(y2r), as_row(y2i)
+    arnoldi_ref[0:1] = as_row(beta * jnp.sqrt(F32(factor)))[:, :half]
+    arnoldi_ref[1:2] = as_row(pr)[:, :half]
+    arnoldi_ref[2:3] = as_row(pi)[:, :half]
+    arnoldi_ref[3:4] = as_row(size_two)[:, :half]
+
+    m1r, m1i, m2r, m2i = (gram[:, k * half : (k + 1) * half] for k in range(4))
+    y1r, y1i, y2r, y2i = (as_row(y)[:, :half] for y in (y1r, y1i, y2r, y2i))
     moment_ref[0] = ((y1r * m1r - y1i * m1i) + (y2r * m2r - y2i * m2i)) * factor
     moment_ref[1] = ((y1r * m1i + y1i * m1r) + (y2r * m2i + y2i * m2r)) * factor
 
@@ -379,8 +387,8 @@
         scratch_shapes=[
             pltpu.VMEM((owned, slots, 2 * width, width), BF16),
             pltpu.VMEM(far_coupling.shape, F32),
-            pltpu.VMEM((owned, 2, groups, rank, width), BF16),
-            pltpu.VMEM((owned, 2, groups, rank, width), BF16),
+            pltpu.VMEM((owned, groups, 2 * rank, width), BF16),
+            pltpu.VMEM((owned, groups, 2 * rank, width), BF16),
             pltpu.VMEM((owned, 2 * width, width), BF16),
             pltpu.VMEM((2, 3 * owned + 1, rows, width), BF16),
             pltpu.VMEM((2, n, owned // per, rows, width), F32),
@@ -391,17 +399,17 @@
             field,
             field,
             field,
+            pltpu.VMEM((n, 1, width), F32),
+            pltpu.VMEM((n, 2, width), F32),
+            pltpu.VMEM((n, 1, width), F32),
             pltpu.VMEM((n, nprobe, width), F32),
-            pltpu.VMEM((n, rows, width), F32),
-            pltpu.VMEM((n, nprobe, width), F32),
-            pltpu.VMEM((n, nprobe + 2 * rows, width), F32),
             pltpu.SemaphoreType.DMA((owned,)),
             pltpu.SemaphoreType.DMA((owned,)),
             pltpu.SemaphoreType.DMA((8, n)),
             pltpu.SemaphoreType.DMA((8, n)),
         ],
         compiler_params=pltpu.CompilerParams(
-            collective_id=0, has_side_effects=True, vmem_limit_bytes=52 * 2**20
+            collective_id=0, has_side_effects=True, vmem_limit_bytes=60 * 2**20
         ),
     )(
         near_list,

time: 65.7 us -> 59.3 us (0.903)
  local copies, waits for them, and re-layouts: 7.88 us -> 4.12 us
  Pallas kernels: 56.4 us -> 54.3 us
    unnamed x19 -> x3, local copies, waits for them, and re-layouts: 7.88 us -> 4.12 us
    pallas_call x1, Pallas kernels: 56.4 us -> 54.3 us  [shards(): pl.pallas_call(functools.partial(kernel, n), out_shape=(jax.ShapeDtypeStr...]
where the time goes in v2:
time: 59.3 us; the launch traced here: 59.1 us
  Pallas kernels  54.3 us (92%)
  local copies, waits for them, and re-layouts  4.12 us (7%)
  between operations  0.64 us (1%)
    pallas_call x1, Pallas kernels, shards(): pl.pallas_call(functools.partial(kernel, n), out_shape=(jax.ShapeDtypeStr...  54.3 us
    unnamed x3, local copies, waits for them, and re-layouts  4.12 us

profile of v2, /device:TPU:0, one launch (start us, length us, event | category | flops | bytes accessed | tf_op | source)
XLA Modules:
  0.0 59.1 jit_solution(14922308252916963859)
XLA Ops:
  0.6 54.3 %shard_map.121 = (f32[8,32,128]{2,1,0:T(8,128)}, f32[2,16,16]{2,1,0:T(8,128)}, f32[4,16]{1,0:T(4,128)}) custom-call(s32[8,27]{1,0:T(8,128)} %near_list.1, s32[8]{0:T(128)} %near_count.1, s32[8]{0:T(128)} %cluster_rows.1, s32[8,32]{1,0:T(8,128)} %far_list.1, f32[2]{0:T(128)} %weight.1, f32[8,32,128]{2,1,0:T(8,128)} %bitcast.4, ...), custom_call_target="tpu_custom_call" | custom-call | tf_op jit(solution)/shard_map/pallas_call | solution.py:378
  54.9 1.6 %copy.16 = f32[8,2,16,128]{3,2,1,0:T(8,128)} copy(f32[8,2,16,128]{3,2,1,0:T(8,128)} %bitcast.5) | data formatting | bytes 262144
  56.5 1.3 %copy.17 = f32[2,16,16]{2,1,0:T(8,128)} copy(f32[2,16,16]{2,1,0:T(8,128)} %get-tuple-element.13) | data formatting | bytes 4096
  57.8 1.2 %copy.18 = f32[4,16]{1,0:T(4,128)} copy(f32[4,16]{1,0:T(4,128)} %get-tuple-element.14) | data formatting | bytes 512

commit v3 on v2

--- a/solution.py
+++ b/solution.py
@@ -224,7 +224,7 @@
             total[i] = acc
             return carry
 
-        lax.fori_loop(0, owned, near, 0)
+        lax.fori_loop(0, owned, near, 0, unroll=2)
         finish_coef()
 
         def expand(d, carry):
@@ -239,7 +239,7 @@
                     spread[d * owned + g * per + a] = m
             return carry
 
-        lax.fori_loop(0, n, expand, 0)
+        lax.fori_loop(0, n, expand, 0, unroll=4)
 
         def far(i, carry):
             acc_hi = jnp.zeros((2 * rows, 2 * rank), F32)
@@ -269,7 +269,7 @@
             image[i] = jnp.where(lane < cluster_rows[i], joined(prod, half, width), 0.0)
             return carry
 
-        lax.fori_loop(0, owned, far, 0)
+        lax.fori_loop(0, owned, far, 0, unroll=4)
         halo(0, 1, 0, right).wait_send()
         halo(1, 1, 2, left).wait_send()
 

time: 59.3 us -> 63.3 us (1.067)
  Pallas kernels: 54.3 us -> 58.3 us
    pallas_call x1, Pallas kernels: 54.3 us -> 58.3 us  [shards(): pl.pallas_call(functools.partial(kernel, n), out_shape=(jax.ShapeDtypeStr...]
where the time goes in v3:
time: 63.3 us; the launch traced here: 63 us
  Pallas kernels  58.3 us (92%)
  local copies, waits for them, and re-layouts  4.12 us (7%)
  between operations  0.64 us (1%)
    pallas_call x1, Pallas kernels, shards(): pl.pallas_call(functools.partial(kernel, n), out_shape=(jax.ShapeDtypeStr...  58.3 us
    unnamed x3, local copies, waits for them, and re-layouts  4.12 us

profile of v3, /device:TPU:0, one launch (start us, length us, event | category | flops | bytes accessed | tf_op | source)
XLA Modules:
  0.0 63.0 jit_solution(9588460041399322100)
XLA Ops:
  0.6 58.3 %shard_map.121 = (f32[8,32,128]{2,1,0:T(8,128)}, f32[2,16,16]{2,1,0:T(8,128)}, f32[4,16]{1,0:T(4,128)}) custom-call(s32[8,27]{1,0:T(8,128)} %near_list.1, s32[8]{0:T(128)} %near_count.1, s32[8]{0:T(128)} %cluster_rows.1, s32[8,32]{1,0:T(8,128)} %far_list.1, f32[2]{0:T(128)} %weight.1, f32[8,32,128]{2,1,0:T(8,128)} %bitcast.4, ...), custom_call_target="tpu_custom_call" | custom-call | tf_op jit(solution)/shard_map/pallas_call | solution.py:378
  58.9 1.6 %copy.16 = f32[8,2,16,128]{3,2,1,0:T(8,128)} copy(f32[8,2,16,128]{3,2,1,0:T(8,128)} %bitcast.5) | data formatting | bytes 262144
  60.5 1.3 %copy.17 = f32[2,16,16]{2,1,0:T(8,128)} copy(f32[2,16,16]{2,1,0:T(8,128)} %get-tuple-element.13) | data formatting | bytes 4096
  61.8 1.2 %copy.18 = f32[4,16]{1,0:T(4,128)} copy(f32[4,16]{1,0:T(4,128)} %get-tuple-element.14) | data formatting | bytes 512

commit v4 on v2

--- a/solution.py
+++ b/solution.py
@@ -295,11 +295,12 @@
         second[i] = second[i] / size_rows
 
     def moments():
-        m1 = jnp.zeros((rows, rows), F32)
-        m2 = jnp.zeros((rows, rows), F32)
-        for i in range(owned):
-            m1 = m1 + dot_nt(base[i], first[i], lax.Precision.HIGHEST)
-            m2 = m2 + dot_nt(base[i], second[i], lax.Precision.HIGHEST)
+        left = jnp.concatenate([base[i] for i in range(owned)], axis=1)
+        right = jnp.concatenate(
+            [jnp.concatenate([first[i], second[i]], axis=0) for i in range(owned)], axis=1
+        )
+        m = dot_nt(left, right, lax.Precision.HIGHEST)
+        m1, m2 = m[:, :rows], m[:, rows:]
         gram_s[me] = jnp.zeros(gram_s.shape[1:], F32)
         for at, m in ((0, m1), (rows, m2)):
             re = m[:half, :half] + m[half:, half:]

time: 59.3 us -> 59.4 us (level)
  no operation moved by 1% of the time
where the time goes in v4:
time: 59.4 us; the launch traced here: 59.1 us
  Pallas kernels  54.3 us (91%)
  local copies, waits for them, and re-layouts  4.12 us (7%)
  between operations  0.64 us (1%)
    pallas_call x1, Pallas kernels, shards(): pl.pallas_call(functools.partial(kernel, n), out_shape=(jax.ShapeDtypeStr...  54.3 us
    unnamed x3, local copies, waits for them, and re-layouts  4.12 us

profile of v4, /device:TPU:0, one launch (start us, length us, event | category | flops | bytes accessed | tf_op | source)
XLA Modules:
  0.0 59.1 jit_solution(17970517266412630841)
XLA Ops:
  0.6 54.3 %shard_map.121 = (f32[8,32,128]{2,1,0:T(8,128)}, f32[2,16,16]{2,1,0:T(8,128)}, f32[4,16]{1,0:T(4,128)}) custom-call(s32[8,27]{1,0:T(8,128)} %near_list.1, s32[8]{0:T(128)} %near_count.1, s32[8]{0:T(128)} %cluster_rows.1, s32[8,32]{1,0:T(8,128)} %far_list.1, f32[2]{0:T(128)} %weight.1, f32[8,32,128]{2,1,0:T(8,128)} %bitcast.4, ...), custom_call_target="tpu_custom_call" | custom-call | tf_op jit(solution)/shard_map/pallas_call | solution.py:379
  55.0 1.6 %copy.16 = f32[8,2,16,128]{3,2,1,0:T(8,128)} copy(f32[8,2,16,128]{3,2,1,0:T(8,128)} %bitcast.5) | data formatting | bytes 262144
  56.5 1.3 %copy.17 = f32[2,16,16]{2,1,0:T(8,128)} copy(f32[2,16,16]{2,1,0:T(8,128)} %get-tuple-element.13) | data formatting | bytes 4096
  57.9 1.2 %copy.18 = f32[4,16]{1,0:T(4,128)} copy(f32[4,16]{1,0:T(4,128)} %get-tuple-element.14) | data formatting | bytes 512
